TPU v7x, 32 devices: a whole 2x2x4 slice. The times are simulated.
32 devices in a mesh: day: 16 (over z, y, x), space: 2 (over core).
Axes of the slice: x: 2, y: 2, z: 4, core: 2. Of those that a mesh axis runs over, the one named last changes fastest.
Arguments:
- latent_start: float32 [16, 6144], P('day', 'space'), may hold values from -3 to 3
- counts: int32 [16, 6144], P('day', 'space'), may hold values from 0 to 24
- log_exposure: float32 [16, 6144], P('day', 'space'), may hold values from -2.5 to 2.5
- time_rate: float32 [6144], P('space'), may hold values from 0.5 to 8
- diag_blocks: float32 [48, 128, 128], P('space'), may hold values from -0.008 to 6, as said below
- upper_blocks: float32 [48, 128, 128], P('space'), may hold values from -0.004 to 0.004
- columns: int32 [48], P('space'), may hold values from 0 to 47, as said below
- inverse_panels: float32 [48, 128, 128], P('space'), may hold values from -0.001 to 0.4, as said below
Outputs:
- latent: float32 [16, 6144], P('day', 'space')
- gradient: float32 [16, 6144], P('day', 'space')
Inputs may be any that keep to these rules, and one draw needn't show every extreme that they name: Block row r's off-diagonal block column lies in the next aligned group of 24 block rows (for the last group, in that group itself), and the rows of one group name distinct columns. `diag_blocks`: Symmetric; each row's diagonal entry exceeds the sum of magnitudes of its other entries by 1.9 or more. `inverse_panels`: Symmetric; each row's diagonal entry exceeds the sum of magnitudes of its other entries.
All inputs are finite; a program needn't handle non-finite values.
Results may differ from a plain program's by a relative error of at most 0.0003.
Values sent between devices are 32-bit elements; how exact they have to be, the bound alone decides.
A program may use at most 64 MiB of HBM per device.

v0:
```python
import jax
import jax.numpy as jnp
from jax import lax
from jax.sharding import PartitionSpec as P

BLOCK = 128
NEWTON = 2
ITERS = 3


def with_halo(block, sides, width):
    for axis, dim in sides:
        count = lax.axis_size(axis)
        forward = [(i, i + 1) for i in range(count - 1)]
        backward = [(target, source) for source, target in forward]
        low = lax.ppermute(
            lax.slice_in_dim(block, block.shape[dim] - width, None, axis=dim), axis, forward
        )
        high = lax.ppermute(lax.slice_in_dim(block, 0, width, axis=dim), axis, backward)
        block = jnp.concatenate([low, block, high], axis=dim)
    return block


def on_device(
    latent_start,
    counts,
    log_exposure,
    time_rate,
    diag_blocks,
    upper_blocks,
    columns,
    inverse_panels,
):
    highest = lax.Precision.HIGHEST
    local_days, width = latent_start.shape
    group_size = diag_blocks.shape[0]
    space_count = lax.axis_size("space")
    day_count = local_days * lax.axis_size("day")
    day_index = lax.axis_index("day") * local_days + jnp.arange(local_days)
    degree = (
        2.0 - jnp.where(day_index == 0, 1.0, 0.0) - jnp.where(day_index == day_count - 1, 1.0, 0.0)
    )
    degree = degree.astype(jnp.float32)[:, None]
    total_blocks = group_size * space_count
    place_all = (columns[:, None] == jnp.arange(total_blocks)[None, :]).astype(jnp.float32)

    def spatial(vector):
        blocks = vector.reshape(local_days, group_size, BLOCK)
        own_part = jnp.einsum("bij,dbj->dbi", diag_blocks, blocks, precision=highest)
        back_terms = jnp.einsum("bij,dbi->dbj", upper_blocks, blocks, precision=highest)
        gathered = lax.all_gather(blocks, "space", axis=1, tiled=True)
        ahead_src = jnp.take(gathered, columns, axis=1)
        spread = jnp.einsum("gn,dgj->dnj", place_all, back_terms, precision=highest)
        behind = lax.psum_scatter(spread, "space", scatter_dimension=1, tiled=True)
        ahead_part = jnp.einsum("bij,dbj->dbi", upper_blocks, ahead_src, precision=highest)
        return (own_part + ahead_part + behind).reshape(local_days, width)

    def prior(vector):
        padded = with_halo(vector, (("day", 0),), 1)
        temporal = time_rate[None, :] * (degree * vector - padded[:-2] - padded[2:])
        return spatial(vector) + temporal

    def precondition(residual):
        blocks = residual.reshape(local_days, group_size, BLOCK)
        smoothed = jnp.einsum("bij,dbj->dbi", inverse_panels, blocks, precision=highest)
        return smoothed.reshape(local_days, width)

    def smoothed_sum(residual, smoothed):
        return lax.psum(jnp.sum(residual * smoothed), ("day", "space"))

    observed = counts.astype(jnp.float32)
    latent = latent_start
    for newton_step in range(NEWTON):
        weight = jnp.exp(latent + log_exposure)
        right_side = -(prior(latent) + weight - observed)
        update = jnp.zeros_like(latent)
        residual = right_side
        smoothed = precondition(residual)
        direction = smoothed
        rz_now = smoothed_sum(residual, smoothed)
        for inner in range(ITERS):
            image = prior(direction) + weight * direction
            curve_sum = lax.psum(jnp.sum(direction * image), ("day", "space"))
            step_size = rz_now / curve_sum
            update = update + step_size * direction
            residual = residual - step_size * image
            if inner < ITERS - 1:
                smoothed = precondition(residual)
                rz_next = smoothed_sum(residual, smoothed)
                direction = smoothed + rz_next / rz_now * direction
                rz_now = rz_next
        latent = latent + update
    gradient = prior(latent) + jnp.exp(latent + log_exposure) - observed
    return (latent, gradient)


def solution(mesh):
    placed = (
        P("day", "space"),
        P("day", "space"),
        P("day", "space"),
        P("space"),
        P("space", None, None),
        P("space", None, None),
        P("space"),
        P("space", None, None),
    )
    return jax.shard_map(
        on_device,
        mesh=mesh,
        in_specs=placed,
        out_specs=(P("day", "space"), P("day", "space")),
        check_vma=False,
    )
```

profile of v0, /device:TPU:0, one launch (start us, length us, event | category | flops | bytes accessed | tf_op | source)
XLA Modules:
  0.0 666.4 jit_solution(13103968584650069867)
XLA Ops:
  7.3 5.1 collective-permute-start
  13.7 2.1 fusion.32
  16.8 1.8 all_gather.27
  19.3 2.5 fusion.45
  21.8 2.6 fusion.34
  24.4 2.3 reduce-scatter.46.cloned.1.call-done
  27.5 3.9 fusion.10
  31.4 1.4 fusion.28
  32.9 2.6 fusion.30
  35.4 3.6 collective-permute-start.2
  40.4 1.8 all-gather
  44.0 2.5 fusion.46
  46.5 7.6 %reduce-scatter.48.cloned.1.call-done = f32[1,24,128]{2,1,0:T(8,128)} async-done(((f32[1,48,128]{2,1,0:T(8,128)}), f32[1,24,128]{2,1,0:T(8,128)}) %reduce-scatter.48.cloned.1.call-update) | async-done | bytes 12304
  55.5 40.7 %all-reduce.10 = (f32[]{:T(128)}, f32[]{:T(128)}) all-reduce(f32[]{:T(128)} %get-tuple-element.6, f32[]{:T(128)} %get-tuple-element.5), channel_id=1, replica_groups=mesh['day'=16,'space'=2] {'day','space'}, use_global_device_ids=true, to_apply=%region_2.4 | all-reduce | flops 2 | bytes 16 | tf_op jit(solution)/shard_map/psum | solution.py:69
  97.6 4.6 fusion.27
  102.1 40.4 %psum.86 = f32[]{:T(128)} all-reduce(f32[]{:T(128)} %get-tuple-element.21), channel_id=1, replica_groups=mesh['day'=16,'space'=2] {'day','space'}, use_global_device_ids=true, to_apply=%region_7.9 | all-reduce | flops 1 | bytes 8 | tf_op jit(solution)/shard_map/psum | solution.py:69
  143.9 1.8 all-gather.1
  147.1 2.5 fusion.47
  149.7 4.2 collective-permute-start.4
  156.8 2.5 fusion.48
  159.3 6.3 reduce-scatter.50.cloned.1.call-done
  167.0 41.1 %psum.87 = f32[]{:T(128)} all-reduce(f32[]{:T(128)} %get-tuple-element.16), channel_id=1, replica_groups=mesh['day'=16,'space'=2] {'day','space'}, use_global_device_ids=true, to_apply=%region_10.12 | all-reduce | flops 1 | bytes 8 | tf_op jit(solution)/shard_map/psum | solution.py:83
  209.4 4.6 fusion.26
  214.0 40.4 %psum.88 = f32[]{:T(128)} all-reduce(f32[]{:T(128)} %get-tuple-element.23), channel_id=1, replica_groups=mesh['day'=16,'space'=2] {'day','space'}, use_global_device_ids=true, to_apply=%region_12.14 | all-reduce | flops 1 | bytes 8 | tf_op jit(solution)/shard_map/psum | solution.py:69
  255.8 1.8 all-gather.2
  259.0 2.5 fusion.50
  261.6 4.2 collective-permute-start.6
  268.7 2.5 fusion.51
  271.2 6.3 reduce-scatter.52.cloned.1.call-done
  278.9 40.7 %psum.89 = f32[]{:T(128)} all-reduce(f32[]{:T(128)} %multiply_reduce_fusion.4), channel_id=1, replica_groups=mesh['day'=16,'space'=2] {'day','space'}, use_global_device_ids=true, to_apply=%region_15.17 | all-reduce | flops 1 | bytes 8 | tf_op jit(solution)/shard_map/psum | solution.py:83
  322.4 2.5 fusion.24
  324.9 4.2 collective-permute-start.8
  330.4 2.0 all_gather.31
  334.0 2.5 fusion.53
  336.5 6.3 reduce-scatter.54.cloned.1.call-done
  343.6 3.9 fusion.4
  349.0 2.6 fusion.20
  351.5 3.6 collective-permute-start.10
  356.4 1.8 all-gather.3
  359.8 2.5 fusion.54
  362.4 7.1 %reduce-scatter.56.cloned.1.call-done = f32[1,24,128]{2,1,0:T(8,128)} async-done(((f32[1,48,128]{2,1,0:T(8,128)}), f32[1,24,128]{2,1,0:T(8,128)}) %reduce-scatter.56.cloned.1.call-update) | async-done | bytes 12304
  370.8 40.7 %all-reduce.9 = (f32[]{:T(128)}, f32[]{:T(128)}) all-reduce(f32[]{:T(128)} %get-tuple-element.4, f32[]{:T(128)} %get-tuple-element.3), channel_id=1, replica_groups=mesh['day'=16,'space'=2] {'day','space'}, use_global_device_ids=true, to_apply=%region_18.20 | all-reduce | flops 2 | bytes 16 | tf_op jit(solution)/shard_map/psum | solution.py:69
  412.9 4.6 fusion.17
  417.5 40.7 %psum.92 = f32[]{:T(128)} all-reduce(f32[]{:T(128)} %get-tuple-element.25), channel_id=1, replica_groups=mesh['day'=16,'space'=2] {'day','space'}, use_global_device_ids=true, to_apply=%region_23.25 | all-reduce | flops 1 | bytes 8 | tf_op jit(solution)/shard_map/psum | solution.py:69
  459.5 1.8 all-gather.4
  462.7 2.6 fusion.55
  465.3 4.2 collective-permute-start.12
  472.4 2.5 fusion.56
  475.0 6.3 reduce-scatter.58.cloned.1.call-done
  482.6 40.7 %psum.93 = f32[]{:T(128)} all-reduce(f32[]{:T(128)} %get-tuple-element.11), channel_id=1, replica_groups=mesh['day'=16,'space'=2] {'day','space'}, use_global_device_ids=true, to_apply=%region_26.28 | all-reduce | flops 1 | bytes 8 | tf_op jit(solution)/shard_map/psum | solution.py:83
  524.6 4.6 fusion.16
  529.2 40.5 %psum.94 = f32[]{:T(128)} all-reduce(f32[]{:T(128)} %get-tuple-element.27), channel_id=1, replica_groups=mesh['day'=16,'space'=2] {'day','space'}, use_global_device_ids=true, to_apply=%region_28.30 | all-reduce | flops 1 | bytes 8 | tf_op jit(solution)/shard_map/psum | solution.py:69
  571.0 1.8 all-gather.5
  574.2 2.5 fusion.58
  576.8 4.2 collective-permute-start.14
  581.0 1.5 collective-permute-start.15
  584.1 2.5 fusion.59
  586.7 6.3 reduce-scatter.60.cloned.1.call-done
  594.3 40.7 %psum.95 = f32[]{:T(128)} all-reduce(f32[]{:T(128)} %multiply_reduce_fusion), channel_id=1, replica_groups=mesh['day'=16,'space'=2] {'day','space'}, use_global_device_ids=true, to_apply=%region_31.33 | all-reduce | flops 1 | bytes 8 | tf_op jit(solution)/shard_map/psum | solution.py:83
  637.8 2.6 fusion.14
  640.4 4.2 collective-permute-start.16
  645.9 1.8 all_gather.35
  649.2 2.5 fusion.61
  651.8 6.3 reduce-scatter.62.cloned.1.call-done
  (127 shorter events, 46.0 us)
Async XLA Ops:
  7.2 6.5 copy-start
  7.2 9.6 %copy-start.3 = (f32[1,3072]{1,0:T(1,128)S(1)}, f32[1,3072]{1,0:T(1,128)}, u32[]{:S(2)}) copy-start(f32[1,3072]{1,0:T(1,128)} %param.10) | copy-start | bytes 36868
  7.2 8.6 %copy-start.7 = (s32[24]{0:T(128)S(1)}, s32[24]{0:T(128)}, u32[]{:S(2)}) copy-start(s32[24]{0:T(128)} %param.16) | copy-start | bytes 292
  7.2 14.6 %copy-start.1 = (f32[24,128,128]{2,1,0:T(8,128)S(1)}, f32[24,128,128]{2,1,0:T(8,128)}, u32[]{:S(2)}) copy-start(f32[24,128,128]{2,1,0:T(8,128)} %param.14) | copy-start | bytes 4718596
  7.2 19.5 %reduce-scatter.46.cloned.1.call-start = ((), (), s32[]{:S(2)}) async-start(), calls=%async_computation.9 | async-start | bytes 36864
  7.3 20.1 %collective-permute-start = (f32[1,3072]{1,0:T(1,128)}, f32[1,3072]{1,0:T(1,128)S(1)}, u32[]{:S(2)}, u32[]{:S(2)}) collective-permute-start(f32[1,3072]{1,0:T(1,128)} %param.10), channel_id=1, source_target_pairs={{0,2},{2,4},{4,6},{6,8},{8,10},{10,12},{12,14},{14,16},{16,18},{18... | collective-permute-start | bytes 36872 | tf_op jit(solution)/shard_map/ppermute | solution.py:16
  12.4 15.0 %collective-permute-start.1 = (f32[1,3072]{1,0:T(1,128)}, f32[1,3072]{1,0:T(1,128)S(1)}, u32[]{:S(2)}, u32[]{:S(2)}) collective-permute-start(f32[1,3072]{1,0:T(1,128)} %param.10), channel_id=1, source_target_pairs={{2,0},{4,2},{6,4},{8,6},{10,8},{12,10},{14,12},{16,14},{18,16},{20... | collective-permute-start | bytes 36872 | tf_op jit(solution)/shard_map/ppermute | solution.py:19
  16.7 37.4 %reduce-scatter.48.cloned.1.call-start = ((), (), s32[]{:S(2)}) async-start(), calls=%async_computation.10 | async-start | bytes 36864
  19.3 8.1 %copy-start.2 = (f32[3072]{0:T(1024)S(1)}, f32[3072]{0:T(1024)}, u32[]{:S(2)}) copy-start(f32[3072]{0:T(1024)} %param.13) | copy-start | bytes 36868
  19.3 8.1 %copy-start.5 = (s32[1,3072]{1,0:T(1,128)S(1)}, s32[1,3072]{1,0:T(1,128)}, u32[]{:S(2)}) copy-start(s32[1,3072]{1,0:T(1,128)} %param.11) | copy-start | bytes 36868
  19.3 8.1 %copy-start.6 = (f32[1,3072]{1,0:T(1,128)S(1)}, f32[1,3072]{1,0:T(1,128)}, u32[]{:S(2)}) copy-start(f32[1,3072]{1,0:T(1,128)} %param.12) | copy-start | bytes 36868
  35.4 19.4 %collective-permute-start.2 = (f32[1,3072]{1,0:T(1,128)S(1)}, f32[1,3072]{1,0:T(1,128)S(1)}, u32[]{:S(2)}, u32[]{:S(2)}) collective-permute-start(f32[1,3072]{1,0:T(1,128)S(1)} %bitcast.430), channel_id=1, source_target_pairs={{0,2},{2,4},{4,6},{6,8},{8,10},{10,12},{12,14},{14,16},{16,18},{18... | collective-permute-start | bytes 36872 | tf_op jit(solution)/shard_map/ppermute | solution.py:16
  39.1 15.7 %collective-permute-start.3 = (f32[1,3072]{1,0:T(1,128)S(1)}, f32[1,3072]{1,0:T(1,128)S(1)}, u32[]{:S(2)}, u32[]{:S(2)}) collective-permute-start(f32[1,3072]{1,0:T(1,128)S(1)} %bitcast.431), channel_id=1, source_target_pairs={{2,0},{4,2},{6,4},{8,6},{10,8},{12,10},{14,12},{16,14},{18,16},{20... | collective-permute-start | bytes 36872 | tf_op jit(solution)/shard_map/ppermute | solution.py:19
  43.7 121.9 %reduce-scatter.50.cloned.1.call-start = ((), (), s32[]{:S(2)}) async-start(), calls=%async_computation.11 | async-start | bytes 36864
  149.7 16.6 %collective-permute-start.4 = (f32[1,3072]{1,0:T(1,128)S(1)}, f32[1,3072]{1,0:T(1,128)S(1)}, u32[]{:S(2)}, u32[]{:S(2)}) collective-permute-start(f32[1,3072]{1,0:T(1,128)S(1)} %bitcast_add_fusion.10), channel_id=1, source_target_pairs={{0,2},{2,4},{4,6},{6,8},{8,10},{10,12},{12,14},{14,16},{16,18},{18... | collective-permute-start | bytes 36872 | tf_op jit(solution)/shard_map/ppermute | solution.py:16
  153.9 12.4 %collective-permute-start.5 = (f32[1,3072]{1,0:T(1,128)S(1)}, f32[1,3072]{1,0:T(1,128)S(1)}, u32[]{:S(2)}, u32[]{:S(2)}) collective-permute-start(f32[1,3072]{1,0:T(1,128)S(1)} %bitcast_add_fusion.10), channel_id=1, source_target_pairs={{2,0},{4,2},{6,4},{8,6},{10,8},{12,10},{14,12},{16,14},{18,16},{20... | collective-permute-start | bytes 36872 | tf_op jit(solution)/shard_map/ppermute | solution.py:19
  156.7 120.8 %reduce-scatter.52.cloned.1.call-start = ((), (), s32[]{:S(2)}) async-start(), calls=%async_computation.12 | async-start | bytes 36864
  261.6 16.6 %collective-permute-start.6 = (f32[1,3072]{1,0:T(1,128)S(1)}, f32[1,3072]{1,0:T(1,128)S(1)}, u32[]{:S(2)}, u32[]{:S(2)}) collective-permute-start(f32[1,3072]{1,0:T(1,128)S(1)} %bitcast_add_fusion.8), channel_id=1, source_target_pairs={{0,2},{2,4},{4,6},{6,8},{8,10},{10,12},{12,14},{14,16},{16,18},{18... | collective-permute-start | bytes 36872 | tf_op jit(solution)/shard_map/ppermute | solution.py:16
  265.8 12.4 %collective-permute-start.7 = (f32[1,3072]{1,0:T(1,128)S(1)}, f32[1,3072]{1,0:T(1,128)S(1)}, u32[]{:S(2)}, u32[]{:S(2)}) collective-permute-start(f32[1,3072]{1,0:T(1,128)S(1)} %bitcast_add_fusion.8), channel_id=1, source_target_pairs={{2,0},{4,2},{6,4},{8,6},{10,8},{12,10},{14,12},{16,14},{18,16},{20... | collective-permute-start | bytes 36872 | tf_op jit(solution)/shard_map/ppermute | solution.py:19
  268.6 74.2 %reduce-scatter.54.cloned.1.call-start = ((), (), s32[]{:S(2)}) async-start(), calls=%async_computation.13 | async-start | bytes 36864
  324.9 18.6 %collective-permute-start.8 = (f32[1,3072]{1,0:T(1,128)S(1)}, f32[1,3072]{1,0:T(1,128)S(1)}, u32[]{:S(2)}, u32[]{:S(2)}) collective-permute-start(f32[1,3072]{1,0:T(1,128)S(1)} %add_add_fusion.1), channel_id=1, source_target_pairs={{0,2},{2,4},{4,6},{6,8},{8,10},{10,12},{12,14},{14,16},{16,18},{18... | collective-permute-start | bytes 36872 | tf_op jit(solution)/shard_map/ppermute | solution.py:16
  329.1 14.4 %collective-permute-start.9 = (f32[1,3072]{1,0:T(1,128)S(1)}, f32[1,3072]{1,0:T(1,128)S(1)}, u32[]{:S(2)}, u32[]{:S(2)}) collective-permute-start(f32[1,3072]{1,0:T(1,128)S(1)} %add_add_fusion.1), channel_id=1, source_target_pairs={{2,0},{4,2},{6,4},{8,6},{10,8},{12,10},{14,12},{16,14},{18,16},{20... | collective-permute-start | bytes 36872 | tf_op jit(solution)/shard_map/ppermute | solution.py:19
  333.9 35.5 %reduce-scatter.56.cloned.1.call-start = ((), (), s32[]{:S(2)}) async-start(), calls=%async_computation.14 | async-start | bytes 36864
  351.5 18.7 %collective-permute-start.10 = (f32[1,3072]{1,0:T(1,128)S(1)}, f32[1,3072]{1,0:T(1,128)S(1)}, u32[]{:S(2)}, u32[]{:S(2)}) collective-permute-start(f32[1,3072]{1,0:T(1,128)S(1)} %bitcast.426), channel_id=1, source_target_pairs={{0,2},{2,4},{4,6},{6,8},{8,10},{10,12},{12,14},{14,16},{16,18},{18... | collective-permute-start | bytes 36872 | tf_op jit(solution)/shard_map/ppermute | solution.py:16
  355.1 15.0 %collective-permute-start.11 = (f32[1,3072]{1,0:T(1,128)S(1)}, f32[1,3072]{1,0:T(1,128)S(1)}, u32[]{:S(2)}, u32[]{:S(2)}) collective-permute-start(f32[1,3072]{1,0:T(1,128)S(1)} %bitcast.427), channel_id=1, source_target_pairs={{2,0},{4,2},{6,4},{8,6},{10,8},{12,10},{14,12},{16,14},{18,16},{20... | collective-permute-start | bytes 36872 | tf_op jit(solution)/shard_map/ppermute | solution.py:19
  359.8 121.5 %reduce-scatter.58.cloned.1.call-start = ((), (), s32[]{:S(2)}) async-start(), calls=%async_computation.15 | async-start | bytes 36864
  465.3 16.6 %collective-permute-start.12 = (f32[1,3072]{1,0:T(1,128)S(1)}, f32[1,3072]{1,0:T(1,128)S(1)}, u32[]{:S(2)}, u32[]{:S(2)}) collective-permute-start(f32[1,3072]{1,0:T(1,128)S(1)} %bitcast_add_fusion.4), channel_id=1, source_target_pairs={{0,2},{2,4},{4,6},{6,8},{8,10},{10,12},{12,14},{14,16},{16,18},{18... | collective-permute-start | bytes 36872 | tf_op jit(solution)/shard_map/ppermute | solution.py:16
  469.5 12.4 %collective-permute-start.13 = (f32[1,3072]{1,0:T(1,128)S(1)}, f32[1,3072]{1,0:T(1,128)S(1)}, u32[]{:S(2)}, u32[]{:S(2)}) collective-permute-start(f32[1,3072]{1,0:T(1,128)S(1)} %bitcast_add_fusion.4), channel_id=1, source_target_pairs={{2,0},{4,2},{6,4},{8,6},{10,8},{12,10},{14,12},{16,14},{18,16},{20... | collective-permute-start | bytes 36872 | tf_op jit(solution)/shard_map/ppermute | solution.py:19
  472.4 120.6 %reduce-scatter.60.cloned.1.call-start = ((), (), s32[]{:S(2)}) async-start(), calls=%async_computation.16 | async-start | bytes 36864
  576.8 16.9 %collective-permute-start.14 = (f32[1,3072]{1,0:T(1,128)S(1)}, f32[1,3072]{1,0:T(1,128)S(1)}, u32[]{:S(2)}, u32[]{:S(2)}) collective-permute-start(f32[1,3072]{1,0:T(1,128)S(1)} %bitcast_add_fusion.2), channel_id=1, source_target_pairs={{0,2},{2,4},{4,6},{6,8},{8,10},{10,12},{12,14},{14,16},{16,18},{18... | collective-permute-start | bytes 36872 | tf_op jit(solution)/shard_map/ppermute | solution.py:16
  581.0 12.7 %collective-permute-start.15 = (f32[1,3072]{1,0:T(1,128)S(1)}, f32[1,3072]{1,0:T(1,128)S(1)}, u32[]{:S(2)}, u32[]{:S(2)}) collective-permute-start(f32[1,3072]{1,0:T(1,128)S(1)} %bitcast_add_fusion.2), channel_id=1, source_target_pairs={{2,0},{4,2},{6,4},{8,6},{10,8},{12,10},{14,12},{16,14},{18,16},{20... | collective-permute-start | bytes 36872 | tf_op jit(solution)/shard_map/ppermute | solution.py:19
  584.1 74.0 %reduce-scatter.62.cloned.1.call-start = ((), (), s32[]{:S(2)}) async-start(), calls=%async_computation.17 | async-start | bytes 36864
  636.4 22.4 %copy-start.4 = (f32[1,3072]{1,0:T(1,128)}, f32[1,3072]{1,0:T(1,128)S(1)}, u32[]{:S(2)}) copy-start(f32[1,3072]{1,0:T(1,128)S(1)} %add_add_fusion) | copy-start | bytes 36868
  640.4 18.4 %collective-permute-start.16 = (f32[1,3072]{1,0:T(1,128)S(1)}, f32[1,3072]{1,0:T(1,128)S(1)}, u32[]{:S(2)}, u32[]{:S(2)}) collective-permute-start(f32[1,3072]{1,0:T(1,128)S(1)} %add_add_fusion), channel_id=1, source_target_pairs={{0,2},{2,4},{4,6},{6,8},{8,10},{10,12},{12,14},{14,16},{16,18},{18... | collective-permute-start | bytes 36872 | tf_op jit(solution)/shard_map/ppermute | solution.py:16
  644.6 14.2 %collective-permute-start.17 = (f32[1,3072]{1,0:T(1,128)S(1)}, f32[1,3072]{1,0:T(1,128)S(1)}, u32[]{:S(2)}, u32[]{:S(2)}) collective-permute-start(f32[1,3072]{1,0:T(1,128)S(1)} %add_add_fusion), channel_id=1, source_target_pairs={{2,0},{4,2},{6,4},{8,6},{10,8},{12,10},{14,12},{16,14},{18,16},{20... | collective-permute-start | bytes 36872 | tf_op jit(solution)/shard_map/ppermute | solution.py:19
Sparse Core Ops, SparseCore 0:
  16.8 9.8 reduce-scatter.45
  43.8 10.1 reduce-scatter.47
  156.9 8.7 reduce-scatter.49
  268.7 8.7 reduce-scatter.51
  334.1 8.6 reduce-scatter.53
  359.9 9.4 reduce-scatter.55
  472.5 8.7 reduce-scatter.57
  584.2 8.7 reduce-scatter.59
  649.4 8.6 reduce-scatter.61
where the time goes:
time: 678 us; the launch traced here: 666 us
  blocking collectives  423 us (62%)
  matrix products  93.4 us (14%)
  waiting for transfers between devices  54.8 us (8%)
  starting transfers between devices  49.9 us (7%)
  between operations  28.1 us (4%)
  other arithmetic  11.9 us (2%)
    psum x6, blocking collectives, smoothed_sum(): return lax.psum(jnp.sum(residual * smoothed), ('day', 'space'))  243 us
    psum x4, blocking collectives, on_device(): curve_sum = lax.psum(jnp.sum(direction * image), ('day', 'space'))  163 us
    unnamed x18, waiting for transfers between devices  54.8 us
    ppermute x9, starting transfers between devices, with_halo(): lax.ppermute(lax.slice_in_dim(block, block.shape[dim] - width, None, axis...  37.4 us
    dot_general x6, matrix products, precondition(): jnp.einsum('bij,dbj->dbi', inverse_panels, blocks, precision=highest)  26.2 us
    dot_general x9, matrix products, spatial(): jnp.einsum('bij,dbj->dbi', diag_blocks, blocks, precision=highest)  23 us
    dot_general x9, matrix products, spatial(): jnp.einsum('bij,dbj->dbi', upper_blocks, ahead_src, precision=highest)  22.9 us
    all_gather x9, blocking collectives, spatial(): gathered = lax.all_gather(blocks, 'space', axis=1, tiled=True)  16.6 us
  transfers between devices with their start and end apart: 27, of which 9 were waited for; matrix products, arithmetic and copies ran while one was open for 7% of the time, Pallas kernels for 0%

commit v1 on v0

v1 whole, which is shorter than its diff:
```python
import functools

import jax
import jax.numpy as jnp
from jax import lax
from jax.experimental import pallas as pl
from jax.experimental.pallas import tpu as pltpu
from jax.sharding import PartitionSpec as P

BLOCK = 128
NEWTON = 2
ITERS = 3
UNROLL = 4
MESH = pl.DeviceIdType.MESH


def split(value):
    high = value.astype(jnp.bfloat16)
    low = (value - high.astype(jnp.float32)).astype(jnp.bfloat16)
    return high, low


def product(value, weights):
    rows = value.shape[0]
    high, low = split(value)
    left = jnp.concatenate(
        [jnp.concatenate([high, high], axis=1), jnp.concatenate([low, low], axis=1)], axis=0
    )
    out = jnp.dot(left, weights, preferred_element_type=jnp.float32)
    return out[:rows] + out[rows:]


def kernel(
    days,
    spaces,
    group,
    latent_ref,
    counts_ref,
    exposure_ref,
    rate_ref,
    diag_ref,
    upper_ref,
    column_ref,
    inverse_ref,
    panel_ref,
    latent_out,
    gradient_out,
    gath,
    lat,
    expo,
    weight,
    resid,
    smooth,
    direc,
    image,
    dimage,
    update,
    back_tmp,
    back_send,
    field_first,
    field_later,
    back_recv,
    red,
    w_du,
    w_ut,
    w_m,
    gs_sem,
    gr_sem,
    fs_sem,
    fr_sem,
    bs_sem,
    br_sem,
    rs_sem,
    rr_sem,
):
    day = lax.axis_index("day")
    me = lax.axis_index("space")
    last = spaces - 1
    stages = days.bit_length() - 1

    def reverse(index):
        out = index * 0
        for bit in range(stages):
            out = out + ((index // (1 << bit)) % 2) * (days >> (bit + 1))
        return out

    def partner(stage):
        step = days >> (stage + 1)
        return day + step - 2 * step * ((day // step) % 2)

    barrier = pltpu.get_barrier_semaphore()
    for stage in range(stages):
        pl.semaphore_signal(barrier, inc=1, device_id=(partner(stage), me), device_id_type=MESH)
    for offset in range(1, spaces):
        pl.semaphore_signal(
            barrier, inc=1, device_id=(day, lax.rem(me + offset, spaces)), device_id_type=MESH
        )

    place = reverse(day)
    gath[place, 0] = latent_ref[...]
    gath[place, 1] = latent_ref[...] + exposure_ref[...]
    gath[place, 2] = counts_ref[...].astype(jnp.float32)

    pl.semaphore_wait(barrier, stages + spaces - 1)

    def prepare(b):
        high, low = split(diag_ref[b])
        w_du[b, :BLOCK, :BLOCK] = high
        w_du[b, BLOCK:, :BLOCK] = low
        upper = upper_ref[b]
        high, low = split(upper)
        w_du[b, :BLOCK, BLOCK:] = high
        w_du[b, BLOCK:, BLOCK:] = low
        high, low = split(upper.T)
        w_ut[b, :BLOCK] = high
        w_ut[b, BLOCK:] = low
        high, low = split(panel_ref[b])
        w_m[b, :BLOCK] = high
        w_m[b, BLOCK:] = low

    for stage in range(stages):
        rows = 1 << stage
        base = (place // rows) * rows
        held = gath.at[pl.ds(base, rows)]
        copy = pltpu.make_async_remote_copy(
            src_ref=held,
            dst_ref=held,
            send_sem=gs_sem.at[stage],
            recv_sem=gr_sem.at[stage],
            device_id=(partner(stage), me),
            device_id_type=MESH,
        )
        copy.start()
        low, high = group * stage // stages, group * (stage + 1) // stages

        @pl.loop(low, high)
        def _(b):
            prepare(b)

        copy.wait()

    for d in range(days):
        spot = int(format(d, "0%db" % stages)[::-1], 2)
        smooth[:, d, :] = gath[spot, 0]
        expo[:, d, :] = gath[spot, 1]
        resid[:, d, :] = gath[spot, 2]

    def each(body):
        @pl.loop(0, group // UNROLL)
        def _(step):
            for i in range(UNROLL):
                body(step * UNROLL + i)

    rows = lax.broadcasted_iota(jnp.int32, (days, BLOCK), 0)
    first_day, last_day = rows == 0, rows == days - 1
    degree = 2.0 - jnp.where(first_day, 1.0, 0.0) - jnp.where(last_day, 1.0, 0.0)

    def prior(slot):
        field_recv = (field_first, field_later)[slot]
        field = pltpu.make_async_remote_copy(
            src_ref=smooth,
            dst_ref=field_recv,
            send_sem=fs_sem.at[slot],
            recv_sem=fr_sem.at[slot],
            device_id=(day, lax.rem(me + last, spaces)),
            device_id_type=MESH,
        )
        back = pltpu.make_async_remote_copy(
            src_ref=back_send,
            dst_ref=back_recv.at[slot],
            send_sem=bs_sem.at[slot],
            recv_sem=br_sem.at[slot],
            device_id=(day, lax.rem(me + 1, spaces)),
            device_id_type=MESH,
        )

        @pl.when(me > 0)
        def _():
            field.start()

        @pl.when(me == last)
        def _():
            field_recv[...] = smooth[...]

        def own(b):
            value = smooth[b]
            both = product(value, w_du[b])
            before = jnp.where(first_day, 0.0, pltpu.roll(value, 1, 0))
            after = jnp.where(last_day, 0.0, pltpu.roll(value, days - 1, 0))
            image[b] = both[:, :BLOCK] + rate_ref[b] * (degree * value - before - after)
            back_tmp[b] = both[:, BLOCK:]

        each(own)

        def permute(b):
            back_send[b] = back_tmp[inverse_ref[b]]

        each(permute)

        @pl.when(me < last)
        def _():
            back.start()
            field.wait_recv()

        def ahead(b):
            image[b] += product(field_recv[column_ref[b]], w_ut[b])

        each(ahead)

        @pl.when(me > 0)
        def _():
            back.wait_recv()
            image[...] += back_recv[slot]
            field.wait_send()

        @pl.when(me == last)
        def _():
            image[...] += back_send[...]

        @pl.when(me < last)
        def _():
            back.wait_send()

    prior(0)
    lat[...] = smooth[...]
    weight[...] = jnp.exp(expo[...])
    resid[...] = resid[...] - weight[...] - image[...]

    def reduced(slot, parts):
        red[slot, me] = jnp.concatenate(
            parts + [jnp.zeros((8 - len(parts), BLOCK), jnp.float32)], axis=0
        )
        copies = []
        for offset in range(1, spaces):
            mine = red.at[slot, me]
            copies.append(
                pltpu.make_async_remote_copy(
                    src_ref=mine,
                    dst_ref=mine,
                    send_sem=rs_sem.at[slot, offset],
                    recv_sem=rr_sem.at[slot, offset],
                    device_id=(day, lax.rem(me + offset, spaces)),
                    device_id_type=MESH,
                )
            )
        for copy in copies:
            copy.start()
        for copy in copies:
            copy.wait()
        total = red[slot, 0]
        for other in range(1, spaces):
            total = total + red[slot, other]
        sums = jnp.sum(total, axis=1, keepdims=True)
        return [sums[i : i + 1] for i in range(len(parts))]

    def across(value):
        return jnp.sum(jnp.sum(value, axis=0), axis=0, keepdims=True)

    one = jnp.ones((1, 1), jnp.float32)

    @pl.loop(0, NEWTON)
    def _(newton):
        direc[...] = jnp.zeros_like(direc)
        dimage[...] = jnp.zeros_like(dimage)
        update[...] = jnp.zeros_like(update)

        def iterate(inner, carry):
            rz_old, curve_old = carry
            count = newton * ITERS + inner

            def precondition(b):
                smooth[b] = product(resid[b], w_m[b])

            each(precondition)
            prior(1)
            image[...] += weight[...] * smooth[...]
            rz, straight, cross = reduced(
                lax.rem(count, 2),
                [
                    across(resid[...] * smooth[...]),
                    across(smooth[...] * image[...]),
                    across(smooth[...] * dimage[...]),
                ],
            )
            ratio = jnp.where(inner == 0, 0.0, rz / rz_old)
            curve = straight + 2.0 * ratio * cross + ratio * ratio * curve_old
            size = rz / curve
            direc[...] = smooth[...] + ratio * direc[...]
            dimage[...] = image[...] + ratio * dimage[...]
            update[...] += size * direc[...]
            resid[...] -= size * dimage[...]
            return rz, curve

        lax.fori_loop(0, ITERS, iterate, (one, one))
        lat[...] += update[...]
        expo[...] += update[...]
        fresh = jnp.exp(expo[...])
        resid[...] = resid[...] + weight[...] * (1.0 + update[...]) - fresh
        weight[...] = fresh

    mine = lax.broadcasted_iota(jnp.int32, (group, days, BLOCK), 1) == day
    latent_out[...] = jnp.sum(jnp.where(mine, lat[...], 0.0), axis=1)
    gradient_out[...] = -jnp.sum(jnp.where(mine, resid[...], 0.0), axis=1)


def on_device(
    latent_start,
    counts,
    log_exposure,
    time_rate,
    diag_blocks,
    upper_blocks,
    columns,
    inverse_panels,
):
    local_days, width = latent_start.shape
    group = diag_blocks.shape[0]
    spaces = lax.axis_size("space")
    days = local_days * lax.axis_size("day")
    stages = days.bit_length() - 1
    local = columns % group
    match = local[:, None] == jnp.arange(group)[None, :]
    inverse = jnp.sum(jnp.where(match, jnp.arange(group)[:, None], 0), axis=0).astype(jnp.int32)
    field = (group, days, BLOCK)
    vmem = pl.BlockSpec(memory_space=pltpu.VMEM)
    smem = pl.BlockSpec(memory_space=pltpu.SMEM)
    sem = pltpu.SemaphoreType.DMA
    f32, bf16 = jnp.float32, jnp.bfloat16
    shape = (group, BLOCK)
    latent, gradient = pl.pallas_call(
        functools.partial(kernel, days, spaces, group),
        out_shape=[jax.ShapeDtypeStruct(shape, f32)] * 2,
        in_specs=[vmem] * 6 + [smem] * 2 + [vmem],
        out_specs=[vmem] * 2,
        scratch_shapes=[pltpu.VMEM((days, 3) + shape, f32)]
        + [pltpu.VMEM(field, f32)] * 13
        + [pltpu.VMEM((2,) + field, f32)]
        + [
            pltpu.VMEM((2, spaces, 8, BLOCK), f32),
            pltpu.VMEM((group, 2 * BLOCK, 2 * BLOCK), bf16),
            pltpu.VMEM((group, 2 * BLOCK, BLOCK), bf16),
            pltpu.VMEM((group, 2 * BLOCK, BLOCK), bf16),
            sem((stages,)),
            sem((stages,)),
            sem((2,)),
            sem((2,)),
            sem((2,)),
            sem((2,)),
            sem((2, spaces)),
            sem((2, spaces)),
        ],
        compiler_params=pltpu.CompilerParams(
            collective_id=0, has_side_effects=True, vmem_limit_bytes=48 * 1024 * 1024
        ),
    )(
        latent_start.reshape(shape),
        counts.reshape(shape),
        log_exposure.reshape(shape),
        time_rate.reshape(group, 1, BLOCK),
        diag_blocks,
        upper_blocks,
        local,
        inverse,
        inverse_panels,
    )
    return latent.reshape(1, width), gradient.reshape(1, width)


def solution(mesh):
    placed = (
        P("day", "space"),
        P("day", "space"),
        P("day", "space"),
        P("space"),
        P("space", None, None),
        P("space", None, None),
        P("space"),
        P("space", None, None),
    )
    return jax.shard_map(
        on_device,
        mesh=mesh,
        in_specs=placed,
        out_specs=(P("day", "space"), P("day", "space")),
        check_vma=False,
    )
```

time: 678 us -> 63.4 us (0.09); the launches traced: 666 us -> 63 us
  blocking collectives: 423 us -> 0 us
  matrix products: 93.4 us -> 0 us
  waiting for transfers between devices: 54.8 us -> 0 us
  Pallas kernels: 0 us -> 53.3 us
  starting transfers between devices: 49.9 us -> 0 us
  between operations: 28.1 us -> 0.65 us
  other arithmetic: 11.9 us -> 0.76 us
    psum x10 -> x0, blocking collectives: 407 us -> none  [the longest x6 243 us: smoothed_sum(): return lax.psum(jnp.sum(residual * smoothed), ('day', 'space'))]
    dot_general x42 -> x0, matrix products: 93.4 us -> none  [the longest x6 26.2 us: precondition(): jnp.einsum('bij,dbj->dbi', inverse_panels, blocks, precision=highest)]
    unnamed x18 -> x0, waiting for transfers between devices: 54.8 us -> none
    pallas_call x0 -> x1, Pallas kernels: none -> 53.3 us  [on_device(): pl.pallas_call(functools.partial(kernel, days, spaces, group), out_shape=...]
    ppermute x18 -> x0, starting transfers between devices: 49.3 us -> none  [the longest x9 37.4 us: with_halo(): lax.ppermute(lax.slice_in_dim(block, block.shape[dim] - width, None, axis...]
    all_gather x9 -> x0, blocking collectives: 16.6 us -> none  [spatial(): gathered = lax.all_gather(blocks, 'space', axis=1, tiled=True)]
    unnamed x16, local copies, waits for them, and re-layouts: 0.04 us -> 8.25 us
  transfers between devices with their start and end apart: 27 -> 0, of which waited for: 9 -> 0; matrix products, arithmetic and copies ran while one was open for 7% -> 0% of each run, Pallas kernels for 0% -> 0%
where the time goes in v1:
time: 63.4 us; the launch traced here: 63 us
  Pallas kernels  53.3 us (84%)
  local copies, waits for them, and re-layouts  8.25 us (13%)
  other arithmetic  0.76 us (1%)
  between operations  0.65 us (1%)
    pallas_call x1, Pallas kernels, on_device(): pl.pallas_call(functools.partial(kernel, days, spaces, group), out_shape=...  53.3 us
    unnamed x16, local copies, waits for them, and re-layouts  8.25 us

profile of v1, /device:TPU:0, one launch (start us, length us, event | category | flops | bytes accessed | tf_op | source)
XLA Modules:
  0.0 63.0 jit_solution(14914468160035132889)
XLA Ops:
  0.6 0.7 %and_select_fusion.column_ref = s32[24]{0:T(128)S(1)} fusion(s32[24]{0:T(128)} %param.14), kind=kLoop, calls=%fused_computation.2 | loop fusion | flops 144 | bytes 192 | tf_op jit(solution)/shard_map/jit(remainder)/select_n | solution.py:321
  1.3 0.1 select_reduce_fusion.inverse_ref
  1.4 0.0 copy-start
  1.4 1.4 %copy-done = f32[24,128,128]{2,1,0:T(8,128)S(1)} copy-done((f32[24,128,128]{2,1,0:T(8,128)S(1)}, f32[24,128,128]{2,1,0:T(8,128)}, u32[]{:S(2)}) %copy-start) | copy-done | bytes 1572888
  2.8 0.0 copy-start.1
  2.8 1.4 %copy-done.1 = f32[24,128,128]{2,1,0:T(8,128)S(1)} copy-done((f32[24,128,128]{2,1,0:T(8,128)S(1)}, f32[24,128,128]{2,1,0:T(8,128)}, u32[]{:S(2)}) %copy-start.1) | copy-done | bytes 1572888
  4.2 0.0 copy-start.2
  4.2 1.4 %copy-done.2 = f32[24,128,128]{2,1,0:T(8,128)S(1)} copy-done((f32[24,128,128]{2,1,0:T(8,128)S(1)}, f32[24,128,128]{2,1,0:T(8,128)}, u32[]{:S(2)}) %copy-start.2) | copy-done | bytes 1572888
  5.6 0.0 copy-start.3
  5.6 0.7 %copy-done.3 = f32[1,3072]{1,0:T(1,128)S(1)} copy-done((f32[1,3072]{1,0:T(1,128)S(1)}, f32[1,3072]{1,0:T(1,128)}, u32[]{:S(2)}) %copy-start.3) | copy-done | bytes 12312
  6.3 0.0 copy-start.4
  6.3 0.7 %copy-done.4 = s32[1,3072]{1,0:T(1,128)S(1)} copy-done((s32[1,3072]{1,0:T(1,128)S(1)}, s32[1,3072]{1,0:T(1,128)}, u32[]{:S(2)}) %copy-start.4) | copy-done | bytes 12312
  7.0 0.0 copy-start.5
  7.0 0.7 %copy-done.5 = f32[1,3072]{1,0:T(1,128)S(1)} copy-done((f32[1,3072]{1,0:T(1,128)S(1)}, f32[1,3072]{1,0:T(1,128)}, u32[]{:S(2)}) %copy-start.5) | copy-done | bytes 12312
  7.7 0.0 copy-start.6
  7.7 0.7 %copy-done.6 = f32[3072]{0:T(1024)S(1)} copy-done((f32[3072]{0:T(1024)S(1)}, f32[3072]{0:T(1024)}, u32[]{:S(2)}) %copy-start.6) | copy-done | bytes 12312
  8.4 53.3 %shard_map.95 = (f32[24,128]{1,0:T(8,128)S(1)}, f32[24,128]{1,0:T(8,128)S(1)}) custom-call(f32[24,128]{1,0:T(8,128)S(1)} %bitcast.8, s32[24,128]{1,0:T(8,128)S(1)} %bitcast.9, f32[24,128]{1,0:T(8,128)S(1)} %bitcast.10, f32[24,1,128]{2,1,0:T(1,128)S(1)} %bitcast.11, f32[24,128,128]{2,1,0:T(8,128)S(1)} %copy-done, f32[24,128,128]{2,1,0:T(8,128)S(1)} %copy-done.1, ...), custom_call_target="tpu_custom_call" | custom-call | tf_op jit(solution)/shard_map/pallas_call | solution.py:330
  61.8 0.6 copy.12
  62.4 0.6 copy.13
Async XLA Ops:
  1.4 1.4 %copy-start = (f32[24,128,128]{2,1,0:T(8,128)S(1)}, f32[24,128,128]{2,1,0:T(8,128)}, u32[]{:S(2)}) copy-start(f32[24,128,128]{2,1,0:T(8,128)} %diag_ref.1) | copy-start | bytes 4718596
  2.8 1.4 %copy-start.1 = (f32[24,128,128]{2,1,0:T(8,128)S(1)}, f32[24,128,128]{2,1,0:T(8,128)}, u32[]{:S(2)}) copy-start(f32[24,128,128]{2,1,0:T(8,128)} %upper_ref.1) | copy-start | bytes 4718596
  4.2 1.4 %copy-start.2 = (f32[24,128,128]{2,1,0:T(8,128)S(1)}, f32[24,128,128]{2,1,0:T(8,128)}, u32[]{:S(2)}) copy-start(f32[24,128,128]{2,1,0:T(8,128)} %panel_ref.1) | copy-start | bytes 4718596
  5.6 0.7 %copy-start.3 = (f32[1,3072]{1,0:T(1,128)S(1)}, f32[1,3072]{1,0:T(1,128)}, u32[]{:S(2)}) copy-start(f32[1,3072]{1,0:T(1,128)} %param.8) | copy-start | bytes 36868
  6.3 0.7 %copy-start.4 = (s32[1,3072]{1,0:T(1,128)S(1)}, s32[1,3072]{1,0:T(1,128)}, u32[]{:S(2)}) copy-start(s32[1,3072]{1,0:T(1,128)} %param.9) | copy-start | bytes 36868
  7.0 0.7 %copy-start.5 = (f32[1,3072]{1,0:T(1,128)S(1)}, f32[1,3072]{1,0:T(1,128)}, u32[]{:S(2)}) copy-start(f32[1,3072]{1,0:T(1,128)} %param.10) | copy-start | bytes 36868
  7.7 0.7 %copy-start.6 = (f32[3072]{0:T(1024)S(1)}, f32[3072]{0:T(1024)}, u32[]{:S(2)}) copy-start(f32[3072]{0:T(1024)} %param.11) | copy-start | bytes 36868

commit v2 on v1

--- a/solution.py
+++ b/solution.py
@@ -34,17 +34,25 @@
     days,
     spaces,
     group,
+    latent_hbm,
+    counts_hbm,
+    exposure_hbm,
+    rate_hbm,
+    diag_hbm,
+    upper_hbm,
+    column_ref,
+    inverse_ref,
+    panel_hbm,
+    latent_out,
+    gradient_out,
     latent_ref,
     counts_ref,
     exposure_ref,
     rate_ref,
     diag_ref,
     upper_ref,
-    column_ref,
-    inverse_ref,
     panel_ref,
-    latent_out,
-    gradient_out,
+    in_sem,
     gath,
     lat,
     expo,
@@ -88,6 +96,15 @@
         step = days >> (stage + 1)
         return day + step - 2 * step * ((day // step) % 2)
 
+    sources = (latent_hbm, exposure_hbm, counts_hbm, rate_hbm, diag_hbm, upper_hbm, panel_hbm)
+    targets = (latent_ref, exposure_ref, counts_ref, rate_ref, diag_ref, upper_ref, panel_ref)
+    loads = [
+        pltpu.make_async_copy(source, target, in_sem.at[i])
+        for i, (source, target) in enumerate(zip(sources, targets))
+    ]
+    for load in loads:
+        load.start()
+
     barrier = pltpu.get_barrier_semaphore()
     for stage in range(stages):
         pl.semaphore_signal(barrier, inc=1, device_id=(partner(stage), me), device_id_type=MESH)
@@ -97,6 +114,8 @@
         )
 
     place = reverse(day)
+    for load in loads[:3]:
+        load.wait()
     gath[place, 0] = latent_ref[...]
     gath[place, 1] = latent_ref[...] + exposure_ref[...]
     gath[place, 2] = counts_ref[...].astype(jnp.float32)
@@ -131,6 +150,9 @@
             device_id_type=MESH,
         )
         copy.start()
+        if stage == 0:
+            for load in loads[3:]:
+                load.wait()
         low, high = group * stage // stages, group * (stage + 1) // stages
 
         @pl.loop(low, high)
@@ -318,11 +340,13 @@
     spaces = lax.axis_size("space")
     days = local_days * lax.axis_size("day")
     stages = days.bit_length() - 1
-    local = columns % group
+    target = jnp.minimum(lax.axis_index("space") + 1, spaces - 1)
+    local = columns - target * group
     match = local[:, None] == jnp.arange(group)[None, :]
     inverse = jnp.sum(jnp.where(match, jnp.arange(group)[:, None], 0), axis=0).astype(jnp.int32)
     field = (group, days, BLOCK)
     vmem = pl.BlockSpec(memory_space=pltpu.VMEM)
+    hbm = pl.BlockSpec(memory_space=pl.ANY)
     smem = pl.BlockSpec(memory_space=pltpu.SMEM)
     sem = pltpu.SemaphoreType.DMA
     f32, bf16 = jnp.float32, jnp.bfloat16
@@ -330,9 +354,17 @@
     latent, gradient = pl.pallas_call(
         functools.partial(kernel, days, spaces, group),
         out_shape=[jax.ShapeDtypeStruct(shape, f32)] * 2,
-        in_specs=[vmem] * 6 + [smem] * 2 + [vmem],
+        in_specs=[hbm] * 6 + [smem] * 2 + [hbm],
         out_specs=[vmem] * 2,
-        scratch_shapes=[pltpu.VMEM((days, 3) + shape, f32)]
+        scratch_shapes=[
+            pltpu.VMEM(shape, f32),
+            pltpu.VMEM(shape, jnp.int32),
+            pltpu.VMEM(shape, f32),
+            pltpu.VMEM((group, 1, BLOCK), f32),
+        ]
+        + [pltpu.VMEM((group, BLOCK, BLOCK), f32)] * 3
+        + [sem((7,))]
+        + [pltpu.VMEM((days, 3) + shape, f32)]
         + [pltpu.VMEM(field, f32)] * 13
         + [pltpu.VMEM((2,) + field, f32)]
         + [
@@ -350,7 +382,7 @@
             sem((2, spaces)),
         ],
         compiler_params=pltpu.CompilerParams(
-            collective_id=0, has_side_effects=True, vmem_limit_bytes=48 * 1024 * 1024
+            collective_id=0, has_side_effects=True, vmem_limit_bytes=60 * 1024 * 1024
         ),
     )(
         latent_start.reshape(shape),

time: 63.4 us -> 59.2 us (0.934)
  local copies, waits for them, and re-layouts: 8.25 us -> 2.62 us
  Pallas kernels: 53.3 us -> 54.3 us
    unnamed x16 -> x4, local copies, waits for them, and re-layouts: 8.25 us -> 2.62 us
    pallas_call x1, Pallas kernels: 53.3 us -> 54.3 us  [on_device(): pl.pallas_call(functools.partial(kernel, days, spaces, group), out_shape=...]
    select_n x1 -> x0, other arithmetic: 0.67 us -> none  [on_device(): local = columns % group]
    sub x0 -> x1, other arithmetic: none -> 0.66 us  [on_device(): local = columns - target * group]
where the time goes in v2:
time: 59.2 us; the launch traced here: 58.8 us
  Pallas kernels  54.3 us (92%)
  local copies, waits for them, and re-layouts  2.62 us (4%)
  other arithmetic  1.26 us (2%)
  between operations  0.64 us (1%)
    pallas_call x1, Pallas kernels, on_device(): pl.pallas_call(functools.partial(kernel, days, spaces, group), out_shape=...  54.3 us
    unnamed x4, local copies, waits for them, and re-layouts  2.62 us

profile of v2, /device:TPU:0, one launch (start us, length us, event | category | flops | bytes accessed | tf_op | source)
XLA Modules:
  0.0 58.8 jit_solution(2344527211933527066)
XLA Ops:
  0.6 0.7 %broadcast_subtract_fusion.column_ref = s32[24]{0:T(128)S(1)} fusion(s32[24]{0:T(128)} %param.14, s32[]{:T(128)S(6)} %mul.3), kind=kLoop, calls=%fused_computation.2 | loop fusion | flops 24 | bytes 196 | tf_op jit(solution)/shard_map/sub | solution.py:344
  1.3 0.0 copy-start
  1.3 0.6 %select_reduce_fusion.inverse_ref = s32[24]{0:T(128)} fusion(s32[24]{0:T(128)S(1)} %broadcast_subtract_fusion.column_ref), kind=kLoop, calls=%fused_computation | loop fusion | flops 1704 | bytes 192 | tf_op jit(solution)/shard_map/reduce_sum | solution.py:346
  1.9 0.0 copy-done
  1.9 54.3 %shard_map.95 = (f32[24,128]{1,0:T(8,128)}, f32[24,128]{1,0:T(8,128)}) custom-call(f32[24,128]{1,0:T(8,128)} %bitcast.8, s32[24,128]{1,0:T(8,128)} %bitcast.9, f32[24,128]{1,0:T(8,128)} %bitcast.10, f32[24,1,128]{2,1,0:T(1,128)} %bitcast.11, f32[24,128,128]{2,1,0:T(8,128)} %diag_hbm.1, f32[24,128,128]{2,1,0:T(8,128)} %upper_hbm.1, s32[24]{0:T(128)} %copy-done, ...), custom_call_target="tpu_custom_call" | custom-call | tf_op jit(solution)/shard_map/pallas_call | solution.py:354
  56.2 1.3 %copy.12 = f32[1,3072]{1,0:T(1,128)} copy(f32[1,3072]{1,0:T(1,128)} %bitcast.7) | data formatting | bytes 24576
  57.5 1.3 %copy.13 = f32[1,3072]{1,0:T(1,128)} copy(f32[1,3072]{1,0:T(1,128)} %bitcast.6) | data formatting | bytes 24576
Async XLA Ops:
  1.3 0.6 %copy-start = (s32[24]{0:T(128)}, s32[24]{0:T(128)S(1)}, u32[]{:S(2)}) copy-start(s32[24]{0:T(128)S(1)} %broadcast_subtract_fusion.column_ref) | copy-start | bytes 292

commit v3 on v2

--- a/solution.py
+++ b/solution.py
@@ -12,6 +12,11 @@
 ITERS = 3
 UNROLL = 4
 MESH = pl.DeviceIdType.MESH
+
+
+def orders(days):
+    steps = [days >> (stage + 1) for stage in range(days.bit_length() - 1)]
+    return steps, steps[:-2] + steps[:-3:-1]
 
 
 def split(value):
@@ -53,7 +58,8 @@
     upper_ref,
     panel_ref,
     in_sem,
-    gath,
+    gath_a,
+    gath_b,
     lat,
     expo,
     weight,
@@ -85,16 +91,14 @@
     me = lax.axis_index("space")
     last = spaces - 1
     stages = days.bit_length() - 1
-
-    def reverse(index):
-        out = index * 0
-        for bit in range(stages):
-            out = out + ((index // (1 << bit)) % 2) * (days >> (bit + 1))
-        return out
-
-    def partner(stage):
-        step = days >> (stage + 1)
+    cut = group * 2 // 3
+    ways = orders(days)
+
+    def partner(step):
         return day + step - 2 * step * ((day // step) % 2)
+
+    def place_of(index, steps):
+        return sum(((index // step) % 2) << stage for stage, step in enumerate(steps))
 
     sources = (latent_hbm, exposure_hbm, counts_hbm, rate_hbm, diag_hbm, upper_hbm, panel_hbm)
     targets = (latent_ref, exposure_ref, counts_ref, rate_ref, diag_ref, upper_ref, panel_ref)
@@ -106,19 +110,21 @@
         load.start()
 
     barrier = pltpu.get_barrier_semaphore()
-    for stage in range(stages):
-        pl.semaphore_signal(barrier, inc=1, device_id=(partner(stage), me), device_id_type=MESH)
+    for step in ways[0]:
+        pl.semaphore_signal(barrier, inc=1, device_id=(partner(step), me), device_id_type=MESH)
     for offset in range(1, spaces):
         pl.semaphore_signal(
             barrier, inc=1, device_id=(day, lax.rem(me + offset, spaces)), device_id_type=MESH
         )
 
-    place = reverse(day)
+    places = [place_of(day, steps) for steps in ways]
     for load in loads[:3]:
         load.wait()
-    gath[place, 0] = latent_ref[...]
-    gath[place, 1] = latent_ref[...] + exposure_ref[...]
-    gath[place, 2] = counts_ref[...].astype(jnp.float32)
+    start = latent_ref[...] + exposure_ref[...]
+    gath_a[places[0], :group] = latent_ref[...]
+    gath_a[places[0], group:] = start[:cut]
+    gath_b[places[1], : group - cut] = start[cut:]
+    gath_b[places[1], group - cut :] = counts_ref[...].astype(jnp.float32)
 
     pl.semaphore_wait(barrier, stages + spaces - 1)
 
@@ -137,35 +143,47 @@
         w_m[b, :BLOCK] = high
         w_m[b, BLOCK:] = low
 
-    for stage in range(stages):
+    def share(way, stage):
         rows = 1 << stage
-        base = (place // rows) * rows
-        held = gath.at[pl.ds(base, rows)]
-        copy = pltpu.make_async_remote_copy(
+        base = (places[way] // rows) * rows
+        held = (gath_a, gath_b)[way].at[pl.ds(base, rows)]
+        return pltpu.make_async_remote_copy(
             src_ref=held,
             dst_ref=held,
-            send_sem=gs_sem.at[stage],
-            recv_sem=gr_sem.at[stage],
-            device_id=(partner(stage), me),
+            send_sem=gs_sem.at[way, stage],
+            recv_sem=gr_sem.at[way, stage],
+            device_id=(partner(ways[way][stage]), me),
             device_id_type=MESH,
         )
-        copy.start()
-        if stage == 0:
-            for load in loads[3:]:
-                load.wait()
+
+    def unpack(way, spots):
+        for d in range(days):
+            spot = place_of(d, ways[way])
+            if spot in spots:
+                if way == 0:
+                    smooth[:, d, :] = gath_a[spot, :group]
+                    expo[:cut, d, :] = gath_a[spot, group:]
+                else:
+                    expo[cut:, d, :] = gath_b[spot, : group - cut]
+                    resid[:, d, :] = gath_b[spot, group - cut :]
+
+    for way in range(2):
+        share(way, 0).start()
+    for load in loads[3:]:
+        load.wait()
+    for stage in range(stages):
         low, high = group * stage // stages, group * (stage + 1) // stages
 
         @pl.loop(low, high)
         def _(b):
             prepare(b)
 
-        copy.wait()
-
-    for d in range(days):
-        spot = int(format(d, "0%db" % stages)[::-1], 2)
-        smooth[:, d, :] = gath[spot, 0]
-        expo[:, d, :] = gath[spot, 1]
-        resid[:, d, :] = gath[spot, 2]
+        for way in range(2):
+            share(way, stage).wait()
+            if stage + 1 < stages:
+                share(way, stage + 1).start()
+    for way in range(2):
+        unpack(way, range(days))
 
     def each(body):
         @pl.loop(0, group // UNROLL)
@@ -364,7 +382,10 @@
         ]
         + [pltpu.VMEM((group, BLOCK, BLOCK), f32)] * 3
         + [sem((7,))]
-        + [pltpu.VMEM((days, 3) + shape, f32)]
+        + [
+            pltpu.VMEM((days, group + group * 2 // 3, BLOCK), f32),
+            pltpu.VMEM((days, 2 * group - group * 2 // 3, BLOCK), f32),
+        ]
         + [pltpu.VMEM(field, f32)] * 13
         + [pltpu.VMEM((2,) + field, f32)]
         + [
@@ -372,8 +393,8 @@
             pltpu.VMEM((group, 2 * BLOCK, 2 * BLOCK), bf16),
             pltpu.VMEM((group, 2 * BLOCK, BLOCK), bf16),
             pltpu.VMEM((group, 2 * BLOCK, BLOCK), bf16),
-            sem((stages,)),
-            sem((stages,)),
+            sem((2, stages)),
+            sem((2, stages)),
             sem((2,)),
             sem((2,)),
             sem((2,)),

time: 59.2 us -> 57.4 us (0.970)
  Pallas kernels: 54.3 us -> 52.5 us
    pallas_call x1, Pallas kernels: 54.3 us -> 52.5 us  [on_device(): pl.pallas_call(functools.partial(kernel, days, spaces, group), out_shape=...]
where the time goes in v3:
time: 57.4 us; the launch traced here: 57 us
  Pallas kernels  52.5 us (91%)
  local copies, waits for them, and re-layouts  2.62 us (5%)
  other arithmetic  1.26 us (2%)
  between operations  0.64 us (1%)
    pallas_call x1, Pallas kernels, on_device(): pl.pallas_call(functools.partial(kernel, days, spaces, group), out_shape=...  52.5 us
    unnamed x4, local copies, waits for them, and re-layouts  2.62 us

profile of v3, /device:TPU:0, one launch (start us, length us, event | category | flops | bytes accessed | tf_op | source)
XLA Modules:
  0.0 57.0 jit_solution(8568447543747227030)
XLA Ops:
  0.6 0.7 %broadcast_subtract_fusion.column_ref = s32[24]{0:T(128)S(1)} fusion(s32[24]{0:T(128)} %param.14, s32[]{:T(128)S(6)} %mul.3), kind=kLoop, calls=%fused_computation.2 | loop fusion | flops 24 | bytes 196 | tf_op jit(solution)/shard_map/sub | solution.py:362
  1.3 0.0 copy-start
  1.3 0.6 %select_reduce_fusion.inverse_ref = s32[24]{0:T(128)} fusion(s32[24]{0:T(128)S(1)} %broadcast_subtract_fusion.column_ref), kind=kLoop, calls=%fused_computation | loop fusion | flops 1704 | bytes 192 | tf_op jit(solution)/shard_map/reduce_sum | solution.py:364
  1.9 0.0 copy-done
  1.9 52.5 %shard_map.95 = (f32[24,128]{1,0:T(8,128)}, f32[24,128]{1,0:T(8,128)}) custom-call(f32[24,128]{1,0:T(8,128)} %bitcast.8, s32[24,128]{1,0:T(8,128)} %bitcast.9, f32[24,128]{1,0:T(8,128)} %bitcast.10, f32[24,1,128]{2,1,0:T(1,128)} %bitcast.11, f32[24,128,128]{2,1,0:T(8,128)} %diag_hbm.1, f32[24,128,128]{2,1,0:T(8,128)} %upper_hbm.1, s32[24]{0:T(128)} %copy-done, ...), custom_call_target="tpu_custom_call" | custom-call | tf_op jit(solution)/shard_map/pallas_call | solution.py:372
  54.4 1.3 %copy.12 = f32[1,3072]{1,0:T(1,128)} copy(f32[1,3072]{1,0:T(1,128)} %bitcast.7) | data formatting | bytes 24576
  55.7 1.3 %copy.13 = f32[1,3072]{1,0:T(1,128)} copy(f32[1,3072]{1,0:T(1,128)} %bitcast.6) | data formatting | bytes 24576
Async XLA Ops:
  1.3 0.6 %copy-start = (s32[24]{0:T(128)}, s32[24]{0:T(128)S(1)}, u32[]{:S(2)}) copy-start(s32[24]{0:T(128)S(1)} %broadcast_subtract_fusion.column_ref) | copy-start | bytes 292

commit v4 on v3

--- a/solution.py
+++ b/solution.py
@@ -10,7 +10,7 @@
 BLOCK = 128
 NEWTON = 2
 ITERS = 3
-UNROLL = 4
+UNROLL = 24
 MESH = pl.DeviceIdType.MESH
 
 
@@ -188,8 +188,10 @@
     def each(body):
         @pl.loop(0, group // UNROLL)
         def _(step):
-            for i in range(UNROLL):
-                body(step * UNROLL + i)
+            blocks = [step * UNROLL + i for i in range(UNROLL)]
+            for b, stores in [(b, body(b)) for b in blocks]:
+                for ref, value in stores:
+                    ref[b] = value
 
     rows = lax.broadcasted_iota(jnp.int32, (days, BLOCK), 0)
     first_day, last_day = rows == 0, rows == days - 1
@@ -227,13 +229,13 @@
             both = product(value, w_du[b])
             before = jnp.where(first_day, 0.0, pltpu.roll(value, 1, 0))
             after = jnp.where(last_day, 0.0, pltpu.roll(value, days - 1, 0))
-            image[b] = both[:, :BLOCK] + rate_ref[b] * (degree * value - before - after)
-            back_tmp[b] = both[:, BLOCK:]
+            temporal = rate_ref[b] * (degree * value - before - after)
+            return (image, both[:, :BLOCK] + temporal), (back_tmp, both[:, BLOCK:])
 
         each(own)
 
         def permute(b):
-            back_send[b] = back_tmp[inverse_ref[b]]
+            return ((back_send, back_tmp[inverse_ref[b]]),)
 
         each(permute)
 
@@ -243,7 +245,7 @@
             field.wait_recv()
 
         def ahead(b):
-            image[b] += product(field_recv[column_ref[b]], w_ut[b])
+            return ((image, image[b] + product(field_recv[column_ref[b]], w_ut[b])),)
 
         each(ahead)
 
@@ -309,7 +311,7 @@
             count = newton * ITERS + inner
 
             def precondition(b):
-                smooth[b] = product(resid[b], w_m[b])
+                return ((smooth, product(resid[b], w_m[b])),)
 
             each(precondition)
             prior(1)

time: 57.4 us -> 49.3 us (0.86)
  Pallas kernels: 52.5 us -> 44.4 us
    pallas_call x1, Pallas kernels: 52.5 us -> 44.4 us  [on_device(): pl.pallas_call(functools.partial(kernel, days, spaces, group), out_shape=...]
where the time goes in v4:
time: 49.3 us; the launch traced here: 48.9 us
  Pallas kernels  44.4 us (90%)
  local copies, waits for them, and re-layouts  2.62 us (5%)
  other arithmetic  1.26 us (3%)
  between operations  0.64 us (1%)
    pallas_call x1, Pallas kernels, on_device(): pl.pallas_call(functools.partial(kernel, days, spaces, group), out_shape=...  44.4 us
    unnamed x4, local copies, waits for them, and re-layouts  2.62 us

profile of v4, /device:TPU:0, one launch (start us, length us, event | category | flops | bytes accessed | tf_op | source)
XLA Modules:
  0.0 48.9 jit_solution(16865757572414553803)
XLA Ops:
  0.6 0.7 %broadcast_subtract_fusion.column_ref = s32[24]{0:T(128)S(1)} fusion(s32[24]{0:T(128)} %param.14, s32[]{:T(128)S(6)} %mul.3), kind=kLoop, calls=%fused_computation.2 | loop fusion | flops 24 | bytes 196 | tf_op jit(solution)/shard_map/sub | solution.py:364
  1.3 0.0 copy-start
  1.3 0.6 %select_reduce_fusion.inverse_ref = s32[24]{0:T(128)} fusion(s32[24]{0:T(128)S(1)} %broadcast_subtract_fusion.column_ref), kind=kLoop, calls=%fused_computation | loop fusion | flops 1704 | bytes 192 | tf_op jit(solution)/shard_map/reduce_sum | solution.py:366
  1.9 0.0 copy-done
  1.9 44.4 %shard_map.95 = (f32[24,128]{1,0:T(8,128)}, f32[24,128]{1,0:T(8,128)}) custom-call(f32[24,128]{1,0:T(8,128)} %bitcast.8, s32[24,128]{1,0:T(8,128)} %bitcast.9, f32[24,128]{1,0:T(8,128)} %bitcast.10, f32[24,1,128]{2,1,0:T(1,128)} %bitcast.11, f32[24,128,128]{2,1,0:T(8,128)} %diag_hbm.1, f32[24,128,128]{2,1,0:T(8,128)} %upper_hbm.1, s32[24]{0:T(128)} %copy-done, ...), custom_call_target="tpu_custom_call" | custom-call | tf_op jit(solution)/shard_map/pallas_call | solution.py:374
  46.3 1.3 %copy.12 = f32[1,3072]{1,0:T(1,128)} copy(f32[1,3072]{1,0:T(1,128)} %bitcast.7) | data formatting | bytes 24576
  47.6 1.3 %copy.13 = f32[1,3072]{1,0:T(1,128)} copy(f32[1,3072]{1,0:T(1,128)} %bitcast.6) | data formatting | bytes 24576
Async XLA Ops:
  1.3 0.6 %copy-start = (s32[24]{0:T(128)}, s32[24]{0:T(128)S(1)}, u32[]{:S(2)}) copy-start(s32[24]{0:T(128)S(1)} %broadcast_subtract_fusion.column_ref) | copy-start | bytes 292
